TPU v7x, 256 devices: a whole 4x4x8 slice. The times are simulated.
256 devices in a mesh: gy: 32 (over x, y, core), gz: 8 (over z).
Axes of the slice: x: 4, y: 4, z: 8, core: 2. Of those that a mesh axis runs over, the one named last changes fastest.
Arguments:
- spectrum: bfloat16 [2, 8, 8192, 1536], P(None, 'gz', 'gy'), may hold values from -2000 to 2000
- layer_index: int32 [1536], replicated, may hold values from 0 to 7, as said below
- y_bounds: int32 [33], replicated, may hold values from 0 to 8192, as said below
- z_bounds: int32 [9], replicated, may hold values from 0 to 1536, as said below
- vp: bfloat16 [10240, 15360], P('gy', 'gz'), may hold values from 3 to 6
- vs: bfloat16 [10240, 15360], P('gy', 'gz'), may hold values from 1.5 to 3.5
- rho: bfloat16 [10240, 15360], P('gy', 'gz'), may hold values from 2 to 2.796875
Outputs:
- new_vp: float32 [10240, 15360], P('gy', 'gz')
- new_vs: float32 [10240, 15360], P('gy', 'gz')
- new_rho: float32 [10240, 15360], P('gy', 'gz')
Inputs may be any that keep to these rules, and one draw needn't show every extreme that they name: `layer_index`: never falls with depth; the first cell is in layer 0 and the last in layer 7. `y_bounds`: starts at 0 and ends at 8192; each brick row spans from 192 to 320 cells, and in every draw some row spans exactly 320 and some exactly 192. `z_bounds`: starts at 0 and ends at 1536; each brick column spans from 3 * 1536 // (4 * 8) to 240 cells, and in every draw some column spans exactly 240 and some exactly the least.
All inputs are finite; a program needn't handle non-finite values.
Results may differ from a plain program's by a relative error of at most 0.0013.
Values may be sent and summed in bfloat16 or wider, within the bound.
No kernel may reach another device: no remote copies, remote signals or barrier semaphores. Data moves between devices by JAX's collectives and lax.ppermute only.
A program may use at most 128 MiB of HBM per device.

v0:
```python
import math

import jax
import jax.numpy as jnp
from jax import lax
from jax.sharding import PartitionSpec as P

LAYERS = 8


CORRELATION = 8.0
HURST_EXPONENT = 0.1
SPREAD_SIGMA = 0.1
DENSITY_GAIN = 0.8
EPSILON = 1e-06
PRECISE = lax.Precision.HIGHEST


def for_sending(shard):

    def short(part):
        return part.astype(jnp.bfloat16) if part.dtype == jnp.float32 else part

    return jax.tree.map(short, shard)


def signed_waves(pieces):
    position = jnp.arange(pieces, dtype=jnp.int32)
    signed = jnp.where(2 * position < pieces, position, position - pieces)
    return signed.astype(jnp.float32) * (2.0 * math.pi / pieces)


def spread(first_axis, second_axis):
    squares = (
        first_axis[:, None] * first_axis[:, None] + second_axis[None, :] * second_axis[None, :]
    )
    return (1.0 + CORRELATION * CORRELATION * squares) ** (-(HURST_EXPONENT + 1.0) / 2.0)


def slot_table(bounds, capacity, limit):
    pieces = bounds.shape[0] - 1
    slot_index = jnp.arange(pieces * capacity, dtype=jnp.int32)
    owners = slot_index // capacity
    offset = slot_index - owners * capacity
    matches = owners[:, None] == jnp.arange(pieces, dtype=jnp.int32)[None, :]
    starts = jnp.sum(jnp.where(matches, bounds[None, :pieces], 0), axis=1)
    finish = jnp.sum(jnp.where(matches, bounds[None, 1:], 0), axis=1)
    return (jnp.minimum(starts + offset, limit - 1), offset < finish - starts)


def phase_table(row_count, col_count, length, weight):
    product = (
        jnp.arange(row_count, dtype=jnp.int32)[:, None]
        * jnp.arange(col_count, dtype=jnp.int32)[None, :]
        % length
    )
    angles = product.astype(jnp.float32) * (2.0 * math.pi / length)
    return (jnp.cos(angles) * weight, jnp.sin(angles) * weight)


def contract(form, left, right):
    return jnp.einsum(form, left, right, precision=PRECISE)


def section_tables(length):
    inside = 128
    outside = length // inside
    outer_pair = phase_table(outside, outside, outside, 1.0)
    twist_pair = phase_table(outside, inside, length, 1.0)
    inner_pair = phase_table(inside, inside, inside, 1.0 / math.sqrt(length))
    return (outside, inside, outer_pair, twist_pair, inner_pair)


def outer_section(real_part, imag_part, form, outer_pair, twist_pair):
    cos_outer, sin_outer = outer_pair
    twist_cos, twist_sin = twist_pair
    first_real = contract(form, real_part, cos_outer) - contract(form, imag_part, sin_outer)
    first_imag = contract(form, real_part, sin_outer) + contract(form, imag_part, cos_outer)
    return (
        first_real * twist_cos - first_imag * twist_sin,
        first_real * twist_sin + first_imag * twist_cos,
    )


def inner_section(real_part, imag_part, form, inner_pair, keep_imag):
    cos_inner, sin_inner = inner_pair
    out_real = contract(form, real_part, cos_inner) - contract(form, imag_part, sin_inner)
    if keep_imag:
        out_imag = contract(form, real_part, sin_inner) + contract(form, imag_part, cos_inner)
        return (out_real, out_imag)
    return out_real


def inverse_rows(real_part, imag_part):
    leading = real_part.shape[:-1]
    length = real_part.shape[-1]
    outside, inside, outer_pair, twist_pair, inner_pair = section_tables(length)
    real_part = real_part.reshape(leading + (outside, inside))
    imag_part = imag_part.reshape(leading + (outside, inside))
    second_real, second_imag = outer_section(
        real_part, imag_part, "...pk,pq->...qk", outer_pair, twist_pair
    )
    result = inner_section(second_real, second_imag, "...qk,km->...mq", inner_pair, False)
    return result.reshape(leading + (length,))


def depth_to_middle(real_part, imag_part):
    planes, row_count, length = real_part.shape
    outside, inside, outer_pair, twist_pair, inner_pair = section_tables(length)
    real_part = real_part.reshape(planes, row_count, outside, inside)
    imag_part = imag_part.reshape(planes, row_count, outside, inside)
    second_real, second_imag = outer_section(
        real_part, imag_part, "xypk,pq->xyqk", outer_pair, twist_pair
    )
    out_real, out_imag = inner_section(second_real, second_imag, "xyqk,km->xmqy", inner_pair, True)
    return (
        out_real.reshape(planes, length, row_count),
        out_imag.reshape(planes, length, row_count),
    )


def global_factor(local_sum, cell_count):
    total_sum = lax.psum(local_sum, ("gy", "gz"))
    return SPREAD_SIGMA / jnp.sqrt(total_sum / cell_count + EPSILON)


def shards(spectrum, layer_index, y_bounds, z_bounds, vp, vs, rho):
    planes = spectrum.shape[1]
    band_rows = spectrum.shape[2]
    depth_cells = spectrum.shape[3]
    lanes_y = lax.axis_size("gy")
    lanes_z = lax.axis_size("gz")
    all_planes = planes * lanes_z
    total_rows = band_rows * lanes_y
    depth_band = depth_cells // lanes_y
    row_cap = vp.shape[0]
    col_cap = vp.shape[1] // all_planes
    cell_count = all_planes * total_rows * depth_cells
    gy_index = lax.axis_index("gy")
    gz_index = lax.axis_index("gz")
    waves_y = signed_waves(total_rows)
    waves_z = signed_waves(depth_cells)
    taper_all = (layer_index.astype(jnp.float32) + 1.0) / LAYERS
    row_index, row_valid = slot_table(y_bounds, row_cap, total_rows)
    col_index, col_valid = slot_table(z_bounds, col_cap, depth_cells)
    depth_start = gy_index * depth_band
    amplitude = spread(lax.dynamic_slice_in_dim(waves_y, gy_index * band_rows, band_rows), waves_z)
    real_part = spectrum[0].astype(jnp.float32) * amplitude
    imag_part = spectrum[1].astype(jnp.float32) * amplitude
    turned_real, turned_imag = depth_to_middle(real_part, imag_part)
    pencil = inverse_rows(
        lax.all_to_all(
            turned_real.astype(jnp.bfloat16), "gy", split_axis=1, concat_axis=2, tiled=True
        ).astype(turned_real.dtype),
        lax.all_to_all(
            turned_imag.astype(jnp.bfloat16), "gy", split_axis=1, concat_axis=2, tiled=True
        ).astype(turned_imag.dtype),
    )
    taper_band = lax.dynamic_slice_in_dim(taper_all, depth_start, depth_band)
    tapered = pencil * taper_band[None, :, None]
    factor = global_factor(jnp.sum(tapered * tapered), cell_count)
    tapered = tapered * factor
    packed = jnp.take(tapered, row_index, axis=2)
    received = lax.all_to_all(
        for_sending(packed), "gy", split_axis=2, concat_axis=1, tiled=True
    ).astype(packed.dtype)
    brick_rows = jnp.transpose(received, (2, 1, 0))
    packed_cols = jnp.take(brick_rows, col_index, axis=1)
    bricks = lax.all_to_all(
        for_sending(packed_cols), "gz", split_axis=1, concat_axis=2, tiled=True
    ).astype(packed_cols.dtype)
    row_mask = lax.dynamic_slice_in_dim(row_valid, gy_index * row_cap, row_cap)
    col_mask = lax.dynamic_slice_in_dim(col_valid, gz_index * col_cap, col_cap)
    valid_cells = row_mask[:, None, None] & col_mask[None, :, None]
    slots_shape = (row_cap, col_cap, all_planes)
    flat_shape = (row_cap, col_cap * all_planes)
    vp_cells = vp.astype(jnp.float32).reshape(slots_shape)
    vs_cells = vs.astype(jnp.float32).reshape(slots_shape)
    rho_cells = rho.astype(jnp.float32).reshape(slots_shape)
    new_vp = jnp.where(valid_cells, vp_cells * (1.0 + bricks), 0.0).reshape(flat_shape)
    new_vs = jnp.where(valid_cells, vs_cells * (1.0 + bricks), 0.0).reshape(flat_shape)
    new_rho = jnp.where(valid_cells, rho_cells * (1.0 + DENSITY_GAIN * bricks), 0.0).reshape(
        flat_shape
    )
    return (new_vp, new_vs, new_rho)


def solution(mesh):
    return jax.shard_map(
        shards,
        mesh=mesh,
        in_specs=(
            P(None, "gz", "gy", None),
            P(),
            P(),
            P(),
            P("gy", "gz"),
            P("gy", "gz"),
            P("gy", "gz"),
        ),
        out_specs=(P("gy", "gz"), P("gy", "gz"), P("gy", "gz")),
        check_vma=False,
    )
```

profile of v0, /device:TPU:1, one launch (start us, length us, event | category | flops | bytes accessed | tf_op | source)
XLA Modules:
  0.0 432.1 jit_solution(7043079430393543661)
XLA Ops:
  2.8 2.8 convert_multiply_fusion
  5.6 2.1 copy.118
  7.7 3.2 fusion.102
  11.0 3.2 fusion.106
  14.2 2.4 copy.120
  16.6 3.7 convolution_add_fusion
  20.4 2.4 fusion.5
  22.8 2.1 fusion.23
  24.9 2.2 fusion.17
  28.5 8.4 %reduce.3 = bf16[1536,256]{1,0:T(8,128)(2,1)S(1)} reduce(bf16[1536,1,256]{2,1,0:T(2,128)(2,1)S(1)} %bitcast.211, bf16[]{:T(256)} %broadcast.712), dimensions={1}, to_apply=%bitcast.176.reduce_sub_computation | reduce | bytes 1572866
  38.1 8.6 %all-to-all-start = ((bf16[32,2,6144]{2,1,0:T(2,128)(2,1)}), bf16[32,2,6144]{2,1,0:T(2,128)(2,1)S(1)}, u32[]{:S(2)}, u32[]{:S(2)}) async-start(bf16[32,2,6144]{2,1,0:T(2,128)(2,1)} %reshape.624), calls=%async_computation | async-start | bytes 1572864 | tf_op jit(solution)/shard_map/all_to_all | solution.py:152
  46.7 3.2 fusion.21
  51.1 4.1 fusion.18
  56.2 8.0 %reduce.4 = bf16[1536,256]{1,0:T(8,128)(2,1)S(1)} reduce(bf16[1536,1,256]{2,1,0:T(2,128)(2,1)S(1)} %bitcast.212, bf16[]{:T(256)} %broadcast.712), dimensions={1}, to_apply=%bitcast.178.reduce_sub_computation | reduce | bytes 1572866
  66.0 7.8 %all-to-all-start.1 = ((bf16[32,2,6144]{2,1,0:T(2,128)(2,1)}), bf16[32,2,6144]{2,1,0:T(2,128)(2,1)}, u32[]{:S(2)}, u32[]{:S(2)}) async-start(bf16[32,2,6144]{2,1,0:T(2,128)(2,1)} %reshape.626), calls=%async_computation.1 | async-start | bytes 1572864 | tf_op jit(solution)/shard_map/all_to_all | solution.py:155
  76.6 2.0 fusion.59
  79.5 8.3 %all-to-all-done.1 = bf16[32,2,6144]{2,1,0:T(2,128)(2,1)} async-done(((bf16[32,2,6144]{2,1,0:T(2,128)(2,1)}), bf16[32,2,6144]{2,1,0:T(2,128)(2,1)}, u32[]{:S(2)}, u32[]{:S(2)}) %all-to-all-start.1) | async-done | bytes 786464 | tf_op jit(solution)/shard_map/all_to_all | solution.py:155
  87.9 4.9 %reshape.627 = bf16[1536,1,256]{2,1,0:T(2,128)(2,1)S(1)} reshape(bf16[32,2,6144]{2,1,0:T(2,128)(2,1)} %all-to-all-done.1) | data formatting | bytes 1572864
  93.4 2.3 convolution_add_fusion.1
  96.7 1.7 fusion.7
  98.4 2.4 multiply_reduce_fusion
  100.8 77.7 %psum.7 = f32[]{:T(128)} all-reduce(f32[]{:T(128)} %get-tuple-element.34), channel_id=1, replica_groups=mesh['gy'=32,'gz'=8] {'gy','gz'}, use_global_device_ids=true, to_apply=%region_5.6 | all-reduce | flops 1 | bytes 8 | tf_op jit(solution)/shard_map/psum | solution.py:123
  179.2 4.5 %copy.159 = f32[1,48,128,64]{1,3,2,0:T(8,128)} copy(f32[1,48,128,64]{2,3,1,0:T(8,128)S(1)} %get-tuple-element.35) | data formatting | bytes 3145728 | tf_op jit(solution)/shard_map/reshape | solution.py:104
  183.7 2.7 fusion
  186.3 36.2 %gather_fusion = bf16[10240,48]{1,0:T(8,128)(2,1)} fusion(bf16[48,8192]{0,1:T(8,128)(2,1)S(1)} %bitcast.205, s32[10240]{0:T(1024)S(1)} %broadcast_clamp_fusion), kind=kCustom, calls=%fused_computation | custom fusion | bytes 2007040 | tf_op jit(solution)/shard_map/jit(_take)/gather | solution.py:163
  222.5 3.0 copy.139
  225.7 7.8 %copy.140 = bf16[1,48,10240]{1,0,2:T(2,128)(2,1)} copy(bf16[1,48,10240]{2,1,0:T(8,128)(2,1)S(1)} %fusion.6) | data formatting | bytes 1966080 | tf_op jit(solution)/shard_map/convert_element_type | solution.py:22
  233.6 56.0 %reduce.5 = bf16[10240,48]{1,0:T(8,128)(2,1)S(1)} reduce(bf16[10240,1,48]{2,1,0:T(2,128)(2,1)} %bitcast.206, bf16[]{:T(256)} %broadcast.712), dimensions={1}, to_apply=%bitcast.180.reduce_sub_computation | reduce | bytes 1966082
  289.6 4.8 %reshape.628 = bf16[32,2,7680]{2,1,0:T(2,128)(2,1)} reshape(bf16[10240,48]{1,0:T(8,128)(2,1)S(1)} %reduce.5) | data formatting | bytes 1966080
  294.4 5.0 %all-to-all-start.2 = ((bf16[32,2,7680]{2,1,0:T(2,128)(2,1)}), bf16[32,2,7680]{2,1,0:T(2,128)(2,1)S(1)}, u32[]{:S(2)}, u32[]{:S(2)}) async-start(bf16[32,2,7680]{2,1,0:T(2,128)(2,1)} %reshape.628), calls=%async_computation.2 | async-start | bytes 1966080 | tf_op jit(solution)/shard_map/all_to_all | solution.py:164
  299.7 15.8 %all-to-all-done.2 = bf16[32,2,7680]{2,1,0:T(2,128)(2,1)S(1)} async-done(((bf16[32,2,7680]{2,1,0:T(2,128)(2,1)}), bf16[32,2,7680]{2,1,0:T(2,128)(2,1)S(1)}, u32[]{:S(2)}, u32[]{:S(2)}) %all-to-all-start.2) | async-done | bytes 983072 | tf_op jit(solution)/shard_map/all_to_all | solution.py:164
  315.5 8.3 %reshape.629 = bf16[10240,1,48]{2,1,0:T(2,128)(2,1)} reshape(bf16[32,2,7680]{2,1,0:T(2,128)(2,1)S(1)} %all-to-all-done.2) | data formatting | bytes 1966080
  323.8 7.4 %bitcast_convert_fusion = f32[1,48,10240]{1,0,2:T(1,128)} fusion(bf16[10240,1,48]{2,1,0:T(2,128)(2,1)} %reshape.629), kind=kLoop, calls=%fused_computation.271 | loop fusion | flops 491520 | bytes 2949120 | tf_op jit(solution)/shard_map/transpose | solution.py:167
  331.2 4.4 %copy.141 = bf16[1,48,32,320]{3,1,2,0:T(8,128)(2,1)S(1)} copy(f32[1,48,32,320]{1,3,2,0:T(8,128)} %bitcast.207) | data formatting | bytes 2949120 | tf_op jit(solution)/shard_map/transpose | solution.py:167
  335.6 6.4 %gather_fusion.1 = bf16[1920,320]{1,0:T(8,128)(2,1)S(1)} fusion(bf16[320,1536]{0,1:T(8,128)(2,1)S(1)} %bitcast.204, s32[2048]{0:T(1024)S(1)} %pad_clamp_fusion), kind=kCustom, calls=%fused_computation.1 | custom fusion | bytes 2465280 | tf_op jit(solution)/shard_map/jit(_take)/gather | solution.py:168
  342.0 2.0 copy.142
  344.1 2.5 fusion.1
  346.6 6.6 %copy.143 = bf16[320,1920,1]{0,2,1:T(2,128)(2,1)S(1)} copy(bf16[320,1920,1]{1,0,2:T(8,128)(2,1)} %fusion.1) | data formatting | bytes 2457600 | tf_op jit(solution)/shard_map/convert_element_type | solution.py:22
  353.2 11.3 %reduce.6 = bf16[1920,320]{1,0:T(8,128)(2,1)} reduce(bf16[1920,1,320]{2,1,0:T(2,128)(2,1)S(1)} %bitcast.210, bf16[]{:T(256)} %broadcast.712), dimensions={1}, to_apply=%bitcast.182.reduce_sub_computation | reduce | bytes 2457602
  364.4 4.5 %reshape.630 = bf16[8,2,38400]{2,1,0:T(2,128)(2,1)} reshape(bf16[1920,320]{1,0:T(8,128)(2,1)} %reduce.6) | data formatting | bytes 2457600
  369.0 4.7 %all-to-all-start.3 = ((bf16[8,2,38400]{2,1,0:T(2,128)(2,1)}), bf16[8,2,38400]{2,1,0:T(2,128)(2,1)}, u32[]{:S(2)}, u32[]{:S(2)}) async-start(bf16[8,2,38400]{2,1,0:T(2,128)(2,1)} %reshape.630), calls=%async_computation.3 | async-start | bytes 2457600 | tf_op jit(solution)/shard_map/all_to_all | solution.py:169
  379.5 27.3 %all-to-all-done.3 = bf16[8,2,38400]{2,1,0:T(2,128)(2,1)} async-done(((bf16[8,2,38400]{2,1,0:T(2,128)(2,1)}), bf16[8,2,38400]{2,1,0:T(2,128)(2,1)}, u32[]{:S(2)}, u32[]{:S(2)}) %all-to-all-start.3) | async-done | bytes 1228832 | tf_op jit(solution)/shard_map/all_to_all | solution.py:169
  406.8 5.2 %reshape.631 = bf16[1920,1,320]{2,1,0:T(2,128)(2,1)S(1)} reshape(bf16[8,2,38400]{2,1,0:T(2,128)(2,1)} %all-to-all-done.3) | data formatting | bytes 2457600
  412.0 5.9 %multiply_add_fusion = (f32[320,1920,1]{0,2,1:T(1,128)S(1)}, f32[320,1920,1]{0,2,1:T(1,128)S(1)}) fusion(bf16[1920,1,320]{2,1,0:T(2,128)(2,1)S(1)} %reshape.631), kind=kLoop, calls=%fused_computation.10 | loop fusion | flops 2457600 | bytes 6144000 | tf_op jit(solution)/shard_map/add | solution.py:182
  417.9 4.8 %bitcast_select_fusion.1 = (f32[320,1920]{0,1:T(8,128)}, f32[320,1920]{0,1:T(8,128)}, f32[320,1920]{0,1:T(8,128)S(1)}) fusion(bf16[320,1920]{0,1:T(8,128)(2,1)S(1)} %copy-done.5, f32[320,8,240,1]{0,3,2,1:T(1,128)S(1)} %bitcast.209, pred[320,240]{0,1:T(8,128)(4,1)S(1)} %broadcast_and_fusion, bf16[320,1920]{0,1:T(8,128)(2,1)S(1)} %copy-done.4, ...), kind=kLoop, calls=%fused_computation.3 | loop fusion | flops 5529600 | bytes 16051200 | tf_op jit(solution)/shard_map/jit(_where)/select_n | solution.py:181
  422.7 3.3 copy.149
  426.1 3.3 copy.148
  429.4 2.2 copy.150
  (74 shorter events, 20.0 us)
Async XLA Ops:
  16.6 3.8 copy-start.3
  22.8 2.1 copy-start
  22.8 2.1 copy-start.2
  37.0 9.7 %copy-start.1 = (f32[256,12,128]{2,1,0:T(8,128)S(1)}, f32[256,12,128]{2,1,0:T(8,128)}, u32[]{:S(2)}) copy-start(f32[256,12,128]{2,1,0:T(8,128)} %copy-done) | copy-start | bytes 4718596
  38.1 27.9 %all-to-all-start = ((bf16[32,2,6144]{2,1,0:T(2,128)(2,1)}), bf16[32,2,6144]{2,1,0:T(2,128)(2,1)S(1)}, u32[]{:S(2)}, u32[]{:S(2)}) async-start(bf16[32,2,6144]{2,1,0:T(2,128)(2,1)} %reshape.624), calls=%async_computation | async-start | bytes 1572864 | tf_op jit(solution)/shard_map/all_to_all | solution.py:152
  46.7 3.2 copy-start.11
  66.0 21.9 %all-to-all-start.1 = ((bf16[32,2,6144]{2,1,0:T(2,128)(2,1)}), bf16[32,2,6144]{2,1,0:T(2,128)(2,1)}, u32[]{:S(2)}, u32[]{:S(2)}) async-start(bf16[32,2,6144]{2,1,0:T(2,128)(2,1)} %reshape.626), calls=%async_computation.1 | async-start | bytes 1572864 | tf_op jit(solution)/shard_map/all_to_all | solution.py:155
  96.7 1.7 copy-start.13
  222.5 3.0 copy-start.10
  294.4 5.0 %copy-start.12 = (s32[9]{0:T(128)S(1)}, s32[9]{0:T(128)}, u32[]{:S(2)}) copy-start(s32[9]{0:T(128)} %param.10) | copy-start | bytes 112
  294.4 21.1 %all-to-all-start.2 = ((bf16[32,2,7680]{2,1,0:T(2,128)(2,1)}), bf16[32,2,7680]{2,1,0:T(2,128)(2,1)S(1)}, u32[]{:S(2)}, u32[]{:S(2)}) async-start(bf16[32,2,7680]{2,1,0:T(2,128)(2,1)} %reshape.628), calls=%async_computation.2 | async-start | bytes 1966080 | tf_op jit(solution)/shard_map/all_to_all | solution.py:164
  369.0 4.7 %copy-start.7 = (bf16[320,1920]{1,0:T(8,128)(2,1)S(1)}, bf16[320,1920]{1,0:T(8,128)(2,1)}, u32[]{:S(2)}) copy-start(bf16[320,1920]{1,0:T(8,128)(2,1)} %param.11) | copy-start | bytes 3686404
  369.0 37.8 %all-to-all-start.3 = ((bf16[8,2,38400]{2,1,0:T(2,128)(2,1)}), bf16[8,2,38400]{2,1,0:T(2,128)(2,1)}, u32[]{:S(2)}, u32[]{:S(2)}) async-start(bf16[8,2,38400]{2,1,0:T(2,128)(2,1)} %reshape.630), calls=%async_computation.3 | async-start | bytes 2457600 | tf_op jit(solution)/shard_map/all_to_all | solution.py:169
  373.7 1.6 copy-start.8
  375.3 1.6 copy-start.9
  411.9 5.9 %copy-start.4 = (bf16[320,1920]{0,1:T(8,128)(2,1)S(1)}, bf16[320,1920]{0,1:T(8,128)(2,1)}, u32[]{:S(2)}) copy-start(bf16[320,1920]{0,1:T(8,128)(2,1)} %copy.116) | copy-start | bytes 3686404
  411.9 5.9 %copy-start.5 = (bf16[320,1920]{0,1:T(8,128)(2,1)S(1)}, bf16[320,1920]{0,1:T(8,128)(2,1)}, u32[]{:S(2)}) copy-start(bf16[320,1920]{0,1:T(8,128)(2,1)} %copy.145) | copy-start | bytes 3686404
  412.0 5.9 %copy-start.6 = (bf16[320,1920]{0,1:T(8,128)(2,1)S(1)}, bf16[320,1920]{0,1:T(8,128)(2,1)}, u32[]{:S(2)}) copy-start(bf16[320,1920]{0,1:T(8,128)(2,1)} %copy.146) | copy-start | bytes 3686404
where the time goes:
time: 439 us; the launch traced here: 432 us
  local copies, waits for them, and re-layouts  126 us (29%)
  other arithmetic  115 us (26%)
  blocking collectives  77.7 us (18%)
  waiting for transfers between devices  51.4 us (12%)
  matrix products  34.5 us (8%)
  starting transfers between devices  26 us (6%)
    unnamed x4, other arithmetic  83.7 us
    psum x1, blocking collectives, global_factor(): total_sum = lax.psum(local_sum, ('gy', 'gz'))  77.7 us
    unnamed x47, local copies, waits for them, and re-layouts  45.7 us
    gather x2, local copies, waits for them, and re-layouts, shards(): packed = jnp.take(tapered, row_index, axis=2)  39.2 us
    dot_general x14, matrix products, contract(): return jnp.einsum(form, left, right, precision=PRECISE)  34.5 us
    all_to_all x1, waiting for transfers between devices, shards(): lax.all_to_all(for_sending(packed_cols), 'gz', split_axis=1, concat_axis=...  27.3 us
    all_to_all x1, waiting for transfers between devices, shards(): lax.all_to_all(for_sending(packed), 'gy', split_axis=2, concat_axis=1, ti...  15.8 us
    convert_element_type x2, local copies, waits for them, and re-layouts, short(): return part.astype(jnp.bfloat16) if part.dtype == jnp.float32 else part  14.4 us
  transfers between devices with their start and end apart: 4, of which 3 were waited for; matrix products, arithmetic and copies ran while one was open for 7% of the time, Pallas kernels for 0%

commit v1 on v0

v1 whole, which is shorter than its diff:
```python
import functools
import math

import jax
import jax.numpy as jnp
import numpy as np
from jax import lax
from jax.experimental import pallas as pl
from jax.experimental.pallas import tpu as pltpu
from jax.sharding import PartitionSpec as P

LAYERS = 8
CORRELATION = 8.0
HURST_EXPONENT = 0.1
SPREAD_SIGMA = 0.1
DENSITY_GAIN = 0.8
EPSILON = 1e-06

NY, NZ, X = 8192, 1536, 8
GY, GZ = 32, 8
ROWS = NY // GY
BAND = NZ // GY
YCAP, ZCAP = 320, 240
INNER = 128
OUTER = NZ // INNER
RADIX = 8
LONG = NY // RADIX
STEP = YCAP // RADIX
PER = 3
WIDE = 384
SLOT = 256
f32, bf16 = jnp.float32, jnp.bfloat16
MIB = 1024 * 1024


def inner_table():
    angle = 2.0 * np.pi * (np.outer(np.arange(INNER), np.arange(INNER)) % INNER) / INNER
    c, s = np.cos(angle), np.sin(angle)
    return np.block([[c, -s], [s, c]]).astype(bf16)


def depth_twist():
    angle = 2.0 * np.pi * np.outer(np.arange(OUTER), np.arange(INNER)) / NZ
    return np.stack([np.cos(angle), np.sin(angle)], axis=1).reshape(2 * OUTER, INNER).astype(np.float32)


def y_table():
    angle = 2.0 * np.pi * (np.outer(np.arange(LONG), np.arange(LONG)) % LONG) / LONG
    full = np.concatenate([np.cos(angle), -np.sin(angle)], axis=0).astype(bf16)
    return np.ascontiguousarray(full.reshape(2 * LONG, LONG // 256, 256).transpose(1, 0, 2))


def y_twist():
    angle = 2.0 * np.pi * np.outer(np.arange(RADIX), np.arange(LONG)) / NY
    both = np.stack([np.cos(angle), np.sin(angle)], axis=1).astype(np.float32)
    split = both.reshape(2 * RADIX, LONG // ROWS, ROWS).transpose(1, 0, 2)
    return np.ascontiguousarray(split)


def weave_table():
    rows = np.arange(X * 128)
    plane, slot = rows // 128, rows % 128
    full = np.zeros((X * 128, X * 128), np.float32)
    full[rows, slot * X + plane] = 1.0
    return np.ascontiguousarray(full.reshape(X * 128, 4, 256).transpose(1, 0, 2)).astype(bf16)


def four(a):
    (r0, i0), (r1, i1), (r2, i2), (r3, i3) = a
    sr, si, dr, di = r0 + r2, i0 + i2, r0 - r2, i0 - i2
    tr, ti, er, ei = r1 + r3, i1 + i3, r1 - r3, i1 - i3
    return [(sr + tr, si + ti), (dr - ei, di + er), (sr - tr, si - ti), (dr + ei, di - er)]


def three(a):
    (r0, i0), (r1, i1), (r2, i2) = a
    tr, ti = r1 + r2, i1 + i2
    half = math.sqrt(3.0) / 2.0
    er, ei = (r1 - r2) * half, (i1 - i2) * half
    mr, mi = r0 - 0.5 * tr, i0 - 0.5 * ti
    return [(r0 + tr, i0 + ti), (mr - ei, mi + er), (mr + ei, mi - er)]


def twelve(a):
    quarter = [four([a[(4 * i + 3 * j) % 12] for j in range(4)]) for i in range(3)]
    out = [None] * 12
    for v in range(4):
        for u, value in enumerate(three([quarter[i][v] for i in range(3)])):
            out[next(q for q in range(12) if q % 3 == u and q % 4 == v)] = value
    return out


def eight(a):
    even, odd = four(a[0::2]), four(a[1::2])
    h = math.sqrt(0.5)
    (r0, i0), (r1, i1), (r2, i2), (r3, i3) = odd
    turned = [(r0, i0), ((r1 - i1) * h, (r1 + i1) * h), (-i2, r2), ((-r3 - i3) * h, (r3 - i3) * h)]
    first = [(e[0] + t[0], e[1] + t[1]) for e, t in zip(even, turned)]
    last = [(e[0] - t[0], e[1] - t[1]) for e, t in zip(even, turned)]
    return first + last


def depth_kernel(place_ref, spec_ref, twist_ref, table_ref, out_ref, mid_ref, hold_ref):
    first = place_ref[0] * ROWS
    lane = lax.broadcasted_iota(jnp.int32, (16, INNER), 1)
    line = lax.broadcasted_iota(jnp.int32, (16, INNER), 0)

    def rows_at(step, carry):
        at = pl.multiple_of(step * 16, 16)
        ky = first + at + line
        wy = jnp.where(2 * ky < NY, ky, ky - NY).astype(f32) * (2.0 * math.pi / NY)
        wy2 = wy * wy
        values = []
        for p in range(OUTER):
            kz = lane + p * INNER
            wz = jnp.where(2 * kz < NZ, kz, kz - NZ).astype(f32) * (2.0 * math.pi / NZ)
            base = 1.0 + CORRELATION * CORRELATION * (wy2 + wz * wz)
            gain = jnp.exp(jnp.log(base) * (-(HURST_EXPONENT + 1.0) / 2.0)) * (1.0 / math.sqrt(NY * NZ))
            span = pl.ds(p * INNER, INNER)
            values.append(
                (
                    spec_ref[0, pl.ds(at, 16), span].astype(f32) * gain,
                    spec_ref[1, pl.ds(at, 16), span].astype(f32) * gain,
                )
            )
        for q, (re, im) in enumerate(twelve(values)):
            c = twist_ref[pl.ds(2 * q, 1), :]
            s = twist_ref[pl.ds(2 * q + 1, 1), :]
            mid_ref[q, pl.ds(at, 16), pl.ds(0, INNER)] = (re * c - im * s).astype(bf16)
            mid_ref[q, pl.ds(at, 16), pl.ds(INNER, INNER)] = (re * s + im * c).astype(bf16)
        return carry

    lax.fori_loop(0, ROWS // 16, rows_at, 0)
    for q in range(OUTER):
        made = lax.dot_general(
            table_ref[...], mid_ref[q], (((1,), (1,)), ((), ())), preferred_element_type=f32
        )
        for half in range(2):
            for part in range(2):
                hold_ref[half, part, pl.ds(q, INNER, stride=OUTER), :] = made[
                    part * INNER : (part + 1) * INNER, half * 128 : (half + 1) * 128
                ]

    def pack(step, carry):
        at = pl.multiple_of(step * BAND, BAND)
        for part in range(2):
            for half in range(2):
                out_ref[step, pl.ds(part * BAND, BAND), pl.ds(half * 128, 128)] = hold_ref[
                    half, part, pl.ds(at, BAND), :
                ].astype(bf16)
        return carry

    lax.fori_loop(0, GY, pack, 0)


def pieces(value):
    high = value.astype(bf16).astype(f32)
    rest = value - high
    middle = rest.astype(bf16).astype(f32)
    return high, middle, rest - middle


def y_kernel(bounds_ref, in_ref, taper_ref, twist_ref, table_ref, out_ref, mid_ref, field_ref):
    groups = LONG // ROWS

    def turn(low, carry):
        for row in range(0, BAND, 16):
            for col in range(0, ROWS, 128):
                values = []
                for e in range(RADIX):
                    block = groups * e + low
                    values.append(
                        (
                            in_ref[block, pl.ds(row, 16), pl.ds(col, 128)].astype(f32),
                            in_ref[block, pl.ds(BAND + row, 16), pl.ds(col, 128)].astype(f32),
                        )
                    )
                lanes = pl.multiple_of(low * ROWS + col, 128)
                for y1, (re, im) in enumerate(eight(values)):
                    c = twist_ref[low, pl.ds(2 * y1, 1), pl.ds(col, 128)]
                    s = twist_ref[low, pl.ds(2 * y1 + 1, 1), pl.ds(col, 128)]
                    at = pl.ds(y1 * BAND + row, 16)
                    mid_ref[at, pl.ds(lanes, 128)] = (re * c - im * s).astype(bf16)
                    mid_ref[at, pl.ds(pl.multiple_of(lanes + LONG, 128), 128)] = (re * s + im * c).astype(bf16)
        return carry

    lax.fori_loop(0, groups, turn, 0)
    total = jnp.zeros((8, 128), f32)
    taper = taper_ref[...]
    for block in range(LONG // 256):
        made = jnp.dot(mid_ref[...], table_ref[block], preferred_element_type=f32)
        for half in range(2):
            part = made[:, half * 128 : (half + 1) * 128] * taper
            field_ref[2 * block + half] = part
            total = total + jnp.sum((part * part).reshape(RADIX * BAND // 8, 8, 128), axis=0)
    field_ref[LONG // 128] = jnp.zeros((RADIX * BAND, 128), f32)
    sums = jnp.sum(jnp.sum(total, axis=0, keepdims=True), axis=1, keepdims=True)
    high, middle, low = pieces(jnp.broadcast_to(sums, (BAND, 128)))
    lane = lax.broadcasted_iota(jnp.int32, (BAND, 128), 1)
    extra = jnp.where(lane == 125, high, jnp.where(lane == 126, middle, jnp.where(lane == 127, low, 0.0)))

    def window(g, carry):
        start = bounds_ref[g]
        y1_first = lax.rem(start, RADIX)
        y2_first = lax.div(start, RADIX)
        for tile in range(WIDE // 128):
            parts = []
            for y1 in range(tile * PER, min(tile * PER + PER, RADIX)):
                at = y2_first + jnp.where(y1 < y1_first, 1, 0)
                block = lax.div(at, 128)
                shift = lax.rem(at, 128)
                rows = pl.ds(y1 * BAND, BAND)
                both = jnp.where(lane >= shift, field_ref[block, rows, :], field_ref[block + 1, rows, :])
                to = (y1 % PER) * STEP
                parts.append(pltpu.roll(both, lax.rem(to - shift + 128, 128), 1))
            if len(parts) < PER:
                parts.append(extra)
            whole = jnp.where(lane < STEP, parts[0], jnp.where(lane < 2 * STEP, parts[1], parts[2]))
            out_ref[g, :, pl.ds(tile * 128, 128)] = whole.astype(bf16)
        return carry

    lax.fori_loop(0, GY, window, 0)


def brick_kernel(start_ref, bounds_ref, in_ref, out_ref, rows_ref):
    def spread_out(g, carry):
        for tile in range(WIDE // 128):
            part = in_ref[g, :, pl.ds(tile * 128, 128)].astype(f32)
            rows_ref[tile, pl.ds(pl.multiple_of(g * BAND, BAND), BAND), :] = part
        return carry

    lax.fori_loop(0, GY, spread_out, 0)
    rows_ref[:, pl.ds(NZ, SLOT), :] = jnp.zeros((WIDE // 128, SLOT, 128), f32)
    tail = jnp.zeros((16, 128), f32)
    for g in range(GY):
        tail = tail + in_ref[g, pl.ds(0, 16), pl.ds(WIDE - 128, 128)].astype(f32)
    lane16 = lax.broadcasted_iota(jnp.int32, (16, 128), 1)
    sums = jnp.sum(jnp.where(lane16 >= 125, tail, 0.0), axis=1, keepdims=True)[0:1, :]
    high, middle, low = pieces(jnp.broadcast_to(sums, (YCAP, SLOT)))
    lane = lax.broadcasted_iota(jnp.int32, (YCAP, SLOT), 1)
    y1_first = lax.rem(start_ref[0], RADIX)
    r = lax.broadcasted_iota(jnp.int32, (YCAP, WIDE), 0)
    col = lax.broadcasted_iota(jnp.int32, (YCAP, WIDE), 1)
    y1 = (r + y1_first) & (RADIX - 1)
    third = jnp.where(y1 >= 2 * PER, 2, jnp.where(y1 >= PER, 1, 0))
    wanted = third * 128 + (y1 - PER * third) * STEP + (r >> 3)
    choose = jnp.where(col == wanted, 1.0, 0.0).astype(bf16)
    for j in range(GZ):
        at = pl.ds(bounds_ref[j], SLOT)
        picked = jnp.concatenate([rows_ref[tile, at, :] for tile in range(WIDE // 128)], axis=1).astype(bf16)
        made = lax.dot_general(choose, picked, (((1,), (1,)), ((), ())), preferred_element_type=f32)
        made = jnp.where(lane == SLOT - 3, high, made)
        made = jnp.where(lane == SLOT - 2, middle, made)
        made = jnp.where(lane == SLOT - 1, low, made)
        out_ref[j] = made.astype(bf16)


def model_kernel(
    extent_ref, in_ref, weave_ref, vp_ref, vs_ref, rho_ref, new_vp_ref, new_vs_ref, new_rho_ref, factor_ref
):
    step = pl.program_id(0)

    @pl.when(step == 0)
    def _():
        tail = jnp.zeros((16, 128), f32)
        for x in range(X):
            tail = tail + in_ref[x, pl.ds(0, 16), pl.ds(SLOT - 128, 128)].astype(f32)
        lane16 = lax.broadcasted_iota(jnp.int32, (16, 128), 1)
        sums = jnp.sum(jnp.where(lane16 >= 125, tail, 0.0), axis=1, keepdims=True)[0:1, :]
        spread = jnp.broadcast_to(sums, (8, 128))
        factor_ref[...] = SPREAD_SIGMA / jnp.sqrt(spread / (X * NY * NZ) + EPSILON)

    lanes = pl.multiple_of(lax.div(step, 4) * 128, 128)
    planes = jnp.concatenate([in_ref[x, :, pl.ds(lanes, 128)] for x in range(X)], axis=1)
    made = jnp.dot(planes, weave_ref[lax.rem(step, 4)], preferred_element_type=f32)
    row = lax.broadcasted_iota(jnp.int32, (YCAP, 256), 0)
    slot = (lax.broadcasted_iota(jnp.int32, (YCAP, 256), 1) + step * 256) >> 3
    valid = (row < extent_ref[0]) & (slot < extent_ref[1])
    picked = made * factor_ref[0:1, 0:1]
    new_vp_ref[...] = jnp.where(valid, vp_ref[...].astype(f32) * (1.0 + picked), 0.0)
    new_vs_ref[...] = jnp.where(valid, vs_ref[...].astype(f32) * (1.0 + picked), 0.0)
    new_rho_ref[...] = jnp.where(valid, rho_ref[...].astype(f32) * (1.0 + DENSITY_GAIN * picked), 0.0)


SMEM = pl.BlockSpec(memory_space=pltpu.SMEM)
VMEM = pl.BlockSpec(memory_space=pltpu.VMEM)


def depth_stage(place, spec):
    return pl.pallas_call(
        depth_kernel,
        out_shape=jax.ShapeDtypeStruct((GY, 2 * BAND, ROWS), bf16),
        in_specs=[SMEM, VMEM, VMEM, VMEM],
        out_specs=VMEM,
        scratch_shapes=[
            pltpu.VMEM((OUTER, ROWS, 2 * INNER), bf16),
            pltpu.VMEM((2, 2, NZ, 128), f32),
        ],
        compiler_params=pltpu.CompilerParams(vmem_limit_bytes=24 * MIB),
    )(place, spec, depth_twist(), inner_table())


def y_stage(y_bounds, turned, taper):
    return pl.pallas_call(
        y_kernel,
        out_shape=jax.ShapeDtypeStruct((GY, BAND, WIDE), bf16),
        in_specs=[SMEM, VMEM, VMEM, VMEM, VMEM],
        out_specs=VMEM,
        scratch_shapes=[
            pltpu.VMEM((RADIX * BAND, 2 * LONG), bf16),
            pltpu.VMEM((LONG // 128 + 1, RADIX * BAND, 128), f32),
        ],
        compiler_params=pltpu.CompilerParams(vmem_limit_bytes=32 * MIB),
    )(y_bounds, turned, taper, y_twist(), y_table())


def brick_stage(start, z_bounds, windows):
    return pl.pallas_call(
        brick_kernel,
        out_shape=jax.ShapeDtypeStruct((GZ, YCAP, SLOT), bf16),
        in_specs=[SMEM, SMEM, VMEM],
        out_specs=VMEM,
        scratch_shapes=[pltpu.VMEM((WIDE // 128, NZ + SLOT, 128), f32)],
        compiler_params=pltpu.CompilerParams(vmem_limit_bytes=24 * MIB),
    )(start, z_bounds, windows)


def model_stage(extent, bricks, vp, vs, rho):
    flat = X * ZCAP
    wide = pl.BlockSpec((YCAP, 256), lambda i: (0, i))
    return pl.pallas_call(
        model_kernel,
        grid=(-(-flat // 256),),
        out_shape=[jax.ShapeDtypeStruct((YCAP, flat), f32)] * 3,
        in_specs=[
            SMEM,
            pl.BlockSpec((GZ, YCAP, SLOT), lambda i: (0, 0, 0)),
            pl.BlockSpec((4, X * 128, 256), lambda i: (0, 0, 0)),
            wide,
            wide,
            wide,
        ],
        out_specs=[wide] * 3,
        scratch_shapes=[pltpu.VMEM((8, 128), f32)],
        compiler_params=pltpu.CompilerParams(vmem_limit_bytes=32 * MIB),
    )(extent, bricks, weave_table(), vp, vs, rho)


def shards(spectrum, layer_index, y_bounds, z_bounds, vp, vs, rho):
    gy_index = lax.axis_index("gy")
    gz_index = lax.axis_index("gz")
    taper_all = (layer_index.astype(f32) + 1.0) / LAYERS
    taper_band = lax.dynamic_slice_in_dim(taper_all, gy_index * BAND, BAND)
    taper = jnp.broadcast_to(jnp.tile(taper_band, RADIX)[:, None], (RADIX * BAND, 128))
    y_pair = lax.dynamic_slice_in_dim(y_bounds, gy_index, 2)
    z_pair = lax.dynamic_slice_in_dim(z_bounds, gz_index, 2)
    extent = jnp.stack([y_pair[1] - y_pair[0], z_pair[1] - z_pair[0]])

    turned = depth_stage(gy_index.reshape(1), spectrum.reshape(2, ROWS, NZ))
    turned = lax.all_to_all(turned, "gy", 0, 0, tiled=True)
    windows = y_stage(y_bounds, turned, taper)
    windows = lax.all_to_all(windows, "gy", 0, 0, tiled=True)
    bricks = brick_stage(y_pair, z_bounds, windows)
    bricks = lax.all_to_all(bricks, "gz", 0, 0, tiled=True)
    return tuple(model_stage(extent, bricks, vp, vs, rho))


def solution(mesh):
    return jax.shard_map(
        shards,
        mesh=mesh,
        in_specs=(
            P(None, "gz", "gy", None),
            P(),
            P(),
            P(),
            P("gy", "gz"),
            P("gy", "gz"),
            P("gy", "gz"),
        ),
        out_specs=(P("gy", "gz"), P("gy", "gz"), P("gy", "gz")),
        check_vma=False,
    )
```

time: 439 us -> 130 us (0.30); the launches traced: 432 us -> 129 us
  local copies, waits for them, and re-layouts: 126 us -> 10.6 us
  other arithmetic: 115 us -> 0.86 us
  blocking collectives: 77.7 us -> 0 us
  matrix products: 34.5 us -> 0 us
  Pallas kernels: 0 us -> 22 us
  waiting for transfers between devices: 51.4 us -> 71.1 us
  starting transfers between devices: 26 us -> 21.4 us
    unnamed x4 -> x0, other arithmetic: 83.7 us -> none
    psum x1 -> x0, blocking collectives: 77.7 us -> none  [global_factor(): total_sum = lax.psum(local_sum, ('gy', 'gz'))]
    gather x4 -> x0, local copies, waits for them, and re-layouts: 47.7 us -> none  [the longest x2 39.2 us: shards(): packed = jnp.take(tapered, row_index, axis=2)]
    unnamed x47 -> x22, local copies, waits for them, and re-layouts: 45.7 us -> 9.07 us
    dot_general x14 -> x0, matrix products: 34.5 us -> none  [contract(): return jnp.einsum(form, left, right, precision=PRECISE)]
    pallas_call x0 -> x4, Pallas kernels: none -> 22 us  [the longest x1 8.3 us: y_stage(): pl.pallas_call(y_kernel, out_shape=jax.ShapeDtypeStruct((GY, BAND, WIDE),...]
    all_to_all x4 -> x3, waiting for transfers between devices: 51.4 us -> 71.1 us  [the longest x1 30.9 us: shards(): bricks = lax.all_to_all(bricks, 'gz', 0, 0, tiled=True)]
    convert_element_type x6 -> x0, local copies, waits for them, and re-layouts: 16.3 us -> none  [the longest x2 14.4 us: short(): return part.astype(jnp.bfloat16) if part.dtype == jnp.float32 else part]
  transfers between devices with their start and end apart: 4 -> 3, of which waited for: 3 -> 3; matrix products, arithmetic and copies ran while one was open for 7% -> 2% of each run, Pallas kernels for 0% -> 0%
where the time goes in v1:
time: 130 us; the launch traced here: 129 us
  waiting for transfers between devices  71.1 us (55%)
  Pallas kernels  22 us (17%)
  starting transfers between devices  21.4 us (16%)
  local copies, waits for them, and re-layouts  10.6 us (8%)
  between operations  3.31 us (3%)
    all_to_all x1, waiting for transfers between devices, shards(): bricks = lax.all_to_all(bricks, 'gz', 0, 0, tiled=True)  30.9 us
    all_to_all x1, waiting for transfers between devices, shards(): turned = lax.all_to_all(turned, 'gy', 0, 0, tiled=True)  21.8 us
    all_to_all x1, waiting for transfers between devices, shards(): windows = lax.all_to_all(windows, 'gy', 0, 0, tiled=True)  18.4 us
    unnamed x22, local copies, waits for them, and re-layouts  9.07 us
    all_to_all x1, starting transfers between devices, shards(): turned = lax.all_to_all(turned, 'gy', 0, 0, tiled=True)  8.72 us
    all_to_all x1, starting transfers between devices, shards(): bricks = lax.all_to_all(bricks, 'gz', 0, 0, tiled=True)  8.32 us
    pallas_call x1, Pallas kernels, y_stage(): pl.pallas_call(y_kernel, out_shape=jax.ShapeDtypeStruct((GY, BAND, WIDE),...  8.3 us
    pallas_call x1, Pallas kernels, model_stage(): pl.pallas_call(model_kernel, grid=(-(-flat // 256),), out_shape=[jax.Shap...  6.84 us
  transfers between devices with their start and end apart: 3, of which 3 were waited for; matrix products, arithmetic and copies ran while one was open for 2% of the time, Pallas kernels for 0%

profile of v1, /device:TPU:1, one launch (start us, length us, event | category | flops | bytes accessed | tf_op | source)
XLA Modules:
  0.0 129.3 jit_solution(14592885283099028711)
XLA Ops:
  0.6 0.0 copy-start.2
  0.6 1.4 %copy-done.2 = bf16[2,1,256,1536]{3,2,1,0:T(8,128)(2,1)S(1)} copy-done((bf16[2,1,256,1536]{3,2,1,0:T(8,128)(2,1)S(1)}, bf16[2,1,256,1536]{3,2,1,0:T(8,128)(2,1)}, u32[]{:S(2)}) %copy-start.2) | copy-done | bytes 1572888
  2.0 0.0 copy-start.6
  2.0 0.9 copy-done.6
  2.9 0.0 copy-start.8
  3.0 0.7 copy-done.8
  3.7 4.1 %shard_map.139 = bf16[32,96,256]{2,1,0:T(8,128)(2,1)} custom-call(s32[1]{0:T(128)} %bitcast.place_ref, bf16[2,256,1536]{2,1,0:T(8,128)(2,1)S(1)} %bitcast.2, f32[24,128]{1,0:T(8,128)S(1)} %copy-done.8, bf16[256,256]{1,0:T(8,128)(2,1)S(1)} %copy-done.6), custom_call_target="tpu_custom_call" | custom-call | tf_op jit(solution)/shard_map/pallas_call | solution.py:290
  7.7 0.0 copy-start.7
  7.7 0.0 copy-start.9
  7.7 8.7 %all-to-all-start = ((bf16[32,96,256]{2,1,0:T(8,128)(2,1)}), bf16[32,96,256]{2,1,0:T(8,128)(2,1)S(1)}, u32[]{:S(2)}, u32[]{:S(2)}) async-start(bf16[32,96,256]{2,1,0:T(8,128)(2,1)} %shard_map.139), calls=%async_computation | async-start | bytes 3145728 | tf_op jit(solution)/shard_map/all_to_all | solution.py:360
  16.5 0.8 fusion.1
  17.3 0.1 broadcast_in_dim.7
  17.3 21.8 %all-to-all-done.in_ref = bf16[32,96,256]{2,1,0:T(8,128)(2,1)S(1)} async-done(((bf16[32,96,256]{2,1,0:T(8,128)(2,1)}), bf16[32,96,256]{2,1,0:T(8,128)(2,1)S(1)}, u32[]{:S(2)}, u32[]{:S(2)}) %all-to-all-start) | async-done | bytes 1572896 | tf_op jit(solution)/shard_map/all_to_all | solution.py:360
  39.1 0.1 broadcast_in_dim.8.taper_ref
  39.3 0.0 copy-done.7
  39.3 0.0 copy-done.9
  39.3 0.0 copy-start
  39.3 2.2 %copy-done = bf16[4,2048,256]{2,1,0:T(8,128)(2,1)S(1)} copy-done((bf16[4,2048,256]{2,1,0:T(8,128)(2,1)S(1)}, bf16[4,2048,256]{2,1,0:T(8,128)(2,1)}, u32[]{:S(2)}) %copy-start) | copy-done | bytes 4194328
  41.5 8.3 %shard_map.140 = bf16[32,48,384]{2,1,0:T(8,128)(2,1)} custom-call(s32[33]{0:T(128)S(1)} %copy-done.9, bf16[32,96,256]{2,1,0:T(8,128)(2,1)S(1)} %all-to-all-done.in_ref, f32[384,128]{1,0:T(8,128)S(1)} %broadcast_in_dim.8.taper_ref, f32[4,16,256]{2,1,0:T(8,128)S(1)} %copy-done.7, bf16[4,2048,256]{2,1,0:T(8,128)(2,1)S(1)} %copy-done), custom_call_target="tpu_custom_call" | custom-call | tf_op jit(solution)/shard_map/pallas_call | solution.py:304
  49.8 0.0 copy-start.10
  49.8 4.4 %all-to-all-start.1 = ((bf16[32,48,384]{2,1,0:T(8,128)(2,1)}), bf16[32,48,384]{2,1,0:T(8,128)(2,1)S(1)}, u32[]{:S(2)}, u32[]{:S(2)}) async-start(bf16[32,48,384]{2,1,0:T(8,128)(2,1)} %shard_map.140), calls=%async_computation.1 | async-start | bytes 2359296 | tf_op jit(solution)/shard_map/all_to_all | solution.py:362
  54.2 0.1 dynamic_slice.9.start_ref
  54.3 18.4 %all-to-all-done.1.in_ref = bf16[32,48,384]{2,1,0:T(8,128)(2,1)S(1)} async-done(((bf16[32,48,384]{2,1,0:T(8,128)(2,1)}), bf16[32,48,384]{2,1,0:T(8,128)(2,1)S(1)}, u32[]{:S(2)}, u32[]{:S(2)}) %all-to-all-start.1) | async-done | bytes 1179680 | tf_op jit(solution)/shard_map/all_to_all | solution.py:362
  72.6 0.0 copy-done.10
  72.6 2.8 %shard_map.141 = bf16[8,320,256]{2,1,0:T(8,128)(2,1)} custom-call(s32[2]{0:T(128)S(1)} %dynamic_slice.9.start_ref, s32[9]{0:T(128)S(1)} %copy-done.10, bf16[32,48,384]{2,1,0:T(8,128)(2,1)S(1)} %all-to-all-done.1.in_ref), custom_call_target="tpu_custom_call" | custom-call | tf_op jit(solution)/shard_map/pallas_call | solution.py:318
  75.5 0.0 copy-start.1
  75.5 8.3 %all-to-all-start.2 = ((bf16[8,320,256]{2,1,0:T(8,128)(2,1)}), bf16[8,320,256]{2,1,0:T(8,128)(2,1)S(1)}, u32[]{:S(2)}, u32[]{:S(2)}) async-start(bf16[8,320,256]{2,1,0:T(8,128)(2,1)} %shard_map.141), calls=%async_computation.2 | async-start | bytes 2621440 | tf_op jit(solution)/shard_map/all_to_all | solution.py:364
  83.8 0.1 dynamic_slice.10
  83.9 0.6 fusion.3
  85.7 0.6 fusion.2
  87.6 0.1 pad_add_fusion.extent_ref
  87.7 30.9 %all-to-all-done.2.in_ref = bf16[8,320,256]{2,1,0:T(8,128)(2,1)S(1)} async-done(((bf16[8,320,256]{2,1,0:T(8,128)(2,1)}), bf16[8,320,256]{2,1,0:T(8,128)(2,1)S(1)}, u32[]{:S(2)}, u32[]{:S(2)}) %all-to-all-start.2) | async-done | bytes 1310752 | tf_op jit(solution)/shard_map/all_to_all | solution.py:364
  118.6 0.0 copy-done.1
  118.6 0.0 copy-start.3
  118.6 1.3 copy-done.3
  119.9 0.0 copy-start.4
  119.9 1.3 copy-done.4
  121.2 0.0 copy-start.5
  121.2 1.3 copy-done.5
  122.5 6.8 %shard_map.142 = (f32[320,1920]{1,0:T(8,128)}, f32[320,1920]{1,0:T(8,128)}, f32[320,1920]{1,0:T(8,128)}) custom-call(s32[2]{0:T(128)S(1)} %pad_add_fusion.extent_ref, bf16[8,320,256]{2,1,0:T(8,128)(2,1)S(1)} %all-to-all-done.2.in_ref, bf16[4,1024,256]{2,1,0:T(8,128)(2,1)S(1)} %copy-done.1, bf16[320,1920]{1,0:T(8,128)(2,1)S(1)} %copy-done.3, ...), custom_call_target="tpu_custom_call" | custom-call | tf_op jit(solution)/shard_map/pallas_call | solution.py:331
  (1 shorter events, 0.0 us)
Async XLA Ops:
  0.6 1.4 %copy-start.2 = (bf16[2,1,256,1536]{3,2,1,0:T(8,128)(2,1)S(1)}, bf16[2,1,256,1536]{3,2,1,0:T(8,128)(2,1)}, u32[]{:S(2)}) copy-start(bf16[2,1,256,1536]{3,2,1,0:T(8,128)(2,1)} %param.12) | copy-start | bytes 4718596
  2.0 0.9 copy-start.6
  2.9 0.7 copy-start.8
  7.7 31.5 %copy-start.7 = (f32[4,16,256]{2,1,0:T(8,128)S(1)}, f32[4,16,256]{2,1,0:T(8,128)}, u32[]{:S(2)}) copy-start(f32[4,16,256]{2,1,0:T(8,128)} %constant.36.clone.twist_ref) | copy-start | bytes 196612
  7.7 31.5 %copy-start.9 = (s32[33]{0:T(128)S(1)}, s32[33]{0:T(128)}, u32[]{:S(2)}) copy-start(s32[33]{0:T(128)} %bounds_ref.2) | copy-start | bytes 400
  7.7 31.4 %all-to-all-start = ((bf16[32,96,256]{2,1,0:T(8,128)(2,1)}), bf16[32,96,256]{2,1,0:T(8,128)(2,1)S(1)}, u32[]{:S(2)}, u32[]{:S(2)}) async-start(bf16[32,96,256]{2,1,0:T(8,128)(2,1)} %shard_map.139), calls=%async_computation | async-start | bytes 3145728 | tf_op jit(solution)/shard_map/all_to_all | solution.py:360
  39.3 2.2 %copy-start = (bf16[4,2048,256]{2,1,0:T(8,128)(2,1)S(1)}, bf16[4,2048,256]{2,1,0:T(8,128)(2,1)}, u32[]{:S(2)}) copy-start(bf16[4,2048,256]{2,1,0:T(8,128)(2,1)} %constant.37.clone.table_ref) | copy-start | bytes 12582916
  49.8 22.9 %copy-start.10 = (s32[9]{0:T(128)S(1)}, s32[9]{0:T(128)}, u32[]{:S(2)}) copy-start(s32[9]{0:T(128)} %bounds_ref.3) | copy-start | bytes 112
  49.8 22.9 %all-to-all-start.1 = ((bf16[32,48,384]{2,1,0:T(8,128)(2,1)}), bf16[32,48,384]{2,1,0:T(8,128)(2,1)S(1)}, u32[]{:S(2)}, u32[]{:S(2)}) async-start(bf16[32,48,384]{2,1,0:T(8,128)(2,1)} %shard_map.140), calls=%async_computation.1 | async-start | bytes 2359296 | tf_op jit(solution)/shard_map/all_to_all | solution.py:362
  75.5 43.1 %copy-start.1 = (bf16[4,1024,256]{2,1,0:T(8,128)(2,1)S(1)}, bf16[4,1024,256]{2,1,0:T(8,128)(2,1)}, u32[]{:S(2)}) copy-start(bf16[4,1024,256]{2,1,0:T(8,128)(2,1)} %constant.38.clone.weave_ref) | copy-start | bytes 6291460
  75.5 43.1 %all-to-all-start.2 = ((bf16[8,320,256]{2,1,0:T(8,128)(2,1)}), bf16[8,320,256]{2,1,0:T(8,128)(2,1)S(1)}, u32[]{:S(2)}, u32[]{:S(2)}) async-start(bf16[8,320,256]{2,1,0:T(8,128)(2,1)} %shard_map.141), calls=%async_computation.2 | async-start | bytes 2621440 | tf_op jit(solution)/shard_map/all_to_all | solution.py:364
  118.6 1.3 copy-start.3
  119.9 1.3 copy-start.4
  121.2 1.3 copy-start.5
